TPU v7x, 128 devices: a whole 4x4x4 slice. The times are simulated.
128 devices in a mesh: dp: 16 (over x, y), red: 8 (over z, core).
Axes of the slice: x: 4, y: 4, z: 4, core: 2. Of those that a mesh axis runs over, the one named last changes fastest.
Arguments:
- frames: bfloat16 [2048, 48, 1536], P(('dp', 'red')), may hold values from -36 to 36
- cotangent: bfloat16 [2048, 48, 1536], P(('dp', 'red')), may hold values from -6 to 6
- w_in: bfloat16 [1536, 3072], P('red'), may hold values from -0.15625 to 0.15625
- kernel: float32 [31, 1536], replicated, may hold values from -1 to 1
- gain: float32 [1536], replicated, may hold values from 0.25 to 1.75
- lengths: int32 [2048], replicated, may hold values from 1 to 47, as said below
Outputs:
- module_output: bfloat16 [2048, 48, 1536], P(('dp', 'red'))
- frame_gradient: bfloat16 [2048, 48, 1536], P(('dp', 'red'))
- grad_w_in: float32 [1536, 3072], P('red')
- grad_kernel: float32 [31, 1536], replicated
- grad_gain: float32 [1536], replicated
Inputs may be any that keep to these rules, and one draw needn't show every extreme that they name: The slots of each device, in order, form 16 groups of 1 slots. The q-th slot of group j on the device with dp index i and red index r and the q-th slot of group j on the device with dp index (2 j + 1 - i) mod 16 and the same red index have lengths that sum to exactly 48. The slots of dp index 0 all hold at least three quarters of 48 frames, rounded up.
All inputs are finite; a program needn't handle non-finite values.
Results may differ from a plain program's by a relative error of at most 0.0054.
Values may be sent and summed in bfloat16 or wider, within the bound.
A program may use at most 128 MiB of HBM per device.

v0:
```python
import jax
import jax.numpy as jnp
from jax import lax
from jax.sharding import PartitionSpec as P

EPSILON = 1e-05


def normalize(widened_frames):
    center = widened_frames - jnp.mean(widened_frames, axis=-1, keepdims=True)
    inv_std = lax.rsqrt(jnp.mean(center * center, axis=-1, keepdims=True) + EPSILON)
    return (center * inv_std, inv_std)


def block_pass(frames, cotangent, valid_frame_mask, segment, weights, kernel, gain):
    row_count, length, model_width = frames.shape
    tap_count = kernel.shape[0]
    reach = tap_count // 2
    widened_frames = frames.astype(jnp.float32)
    normed, inv_std = normalize(widened_frames)
    scaled = (normed * gain).astype(jnp.bfloat16)
    flat_in = scaled.reshape(row_count * length, model_width)
    hidden = jnp.dot(flat_in, weights, preferred_element_type=jnp.float32)
    hidden = hidden.reshape(row_count, length, 2 * model_width)
    value_portion = hidden[..., :model_width]
    gate_sigmoid = jax.nn.sigmoid(hidden[..., model_width:])
    frame_validity = valid_frame_mask.astype(jnp.float32)[..., None]
    gated_linear_output = value_portion * gate_sigmoid * frame_validity
    padded = jnp.pad(gated_linear_output, ((0, 0), (reach, reach), (0, 0)))
    seg_pad = jnp.pad(segment, ((0, 0), (reach, reach)), constant_values=-1)
    convolved_frames = jnp.zeros_like(gated_linear_output)
    for offset in range(tap_count):
        window = padded[:, offset : offset + length]
        same_seg = (seg_pad[:, offset : offset + length] == segment).astype(jnp.float32)[..., None]
        convolved_frames = convolved_frames + kernel[offset] * (window * same_seg)
    swish_activation = jax.nn.sigmoid(convolved_frames)
    module_output = (
        (widened_frames + convolved_frames * swish_activation) * frame_validity
    ).astype(jnp.bfloat16)
    incoming_gradient = cotangent.astype(jnp.float32) * frame_validity
    grad_conv = incoming_gradient * (
        swish_activation * (1.0 + convolved_frames * (1.0 - swish_activation))
    )
    grad_pad = jnp.pad(grad_conv, ((0, 0), (reach, reach), (0, 0)))
    gated_linear_gradient = jnp.zeros_like(gated_linear_output)
    kernel_terms = []
    for offset in range(tap_count):
        window = padded[:, offset : offset + length]
        same_seg = (seg_pad[:, offset : offset + length] == segment).astype(jnp.float32)[..., None]
        kernel_terms.append(jnp.sum(grad_conv * window * same_seg, axis=(0, 1)))
        back_start = 2 * reach - offset
        back_same = (seg_pad[:, back_start : back_start + length] == segment).astype(jnp.float32)[
            ..., None
        ]
        gated_linear_gradient = gated_linear_gradient + kernel[offset] * (
            grad_pad[:, back_start : back_start + length] * back_same
        )
    gated_linear_gradient = gated_linear_gradient * frame_validity
    grad_hidden = jnp.concatenate(
        [
            gated_linear_gradient * gate_sigmoid,
            gated_linear_gradient * value_portion * gate_sigmoid * (1.0 - gate_sigmoid),
        ],
        axis=-1,
    ).astype(jnp.bfloat16)
    flat_grad = grad_hidden.reshape(row_count * length, 2 * model_width)
    grad_scaled = lax.dot_general(
        flat_grad, weights, (((1,), (1,)), ((), ())), preferred_element_type=jnp.float32
    )
    grad_scaled = grad_scaled.reshape(row_count, length, model_width)
    gain_term = jnp.sum(grad_scaled * normed, axis=(0, 1))
    grad_normed = grad_scaled * gain
    frame_gradient = incoming_gradient + inv_std * (
        grad_normed
        - jnp.mean(grad_normed, axis=-1, keepdims=True)
        - normed * jnp.mean(grad_normed * normed, axis=-1, keepdims=True)
    )
    frame_gradient = (frame_gradient * frame_validity).astype(jnp.bfloat16)
    return (module_output, frame_gradient, flat_in, flat_grad, jnp.stack(kernel_terms), gain_term)


def local(frames, cotangent, w_in, kernel, gain, lengths):
    dp_size = lax.axis_size("dp")
    red_size = lax.axis_size("red")
    dp_index = lax.axis_index("dp")
    red_index = lax.axis_index("red")
    local_utts, length, model_width = frames.shape
    weights = lax.all_gather(w_in, "red", axis=0, tiled=True)
    positions = jnp.arange(length, dtype=jnp.int32)
    by_owner = lengths.reshape(dp_size, red_size, local_utts)
    own_lengths = lax.dynamic_slice(by_owner, (dp_index, red_index, 0), (1, 1, local_utts)).reshape(
        local_utts
    )
    valid_frame_mask = positions[None, :] < own_lengths[:, None]
    segment = jnp.where(valid_frame_mask, 0, 1).astype(jnp.int32)
    module_output, frame_gradient, flat_in, flat_grad, kernel_part, gain_part = block_pass(
        frames, cotangent, valid_frame_mask, segment, weights, kernel, gain
    )
    grad_scale = lax.rsqrt(jnp.sum(lengths).astype(jnp.float32))
    block_rows = model_width // (dp_size * red_size)
    ordered = flat_in.reshape(-1, red_size, dp_size, block_rows)
    ordered = jnp.transpose(ordered, (0, 2, 1, 3)).reshape(-1, model_width)
    owned_rows = lax.psum_scatter(
        lax.dot_general(
            ordered, flat_grad, (((0,), (0,)), ((), ())), preferred_element_type=jnp.float32
        ),
        ("dp", "red"),
        scatter_dimension=0,
        tiled=True,
    )
    grad_weights = lax.all_gather(owned_rows, "dp", axis=0, tiled=True)
    kernel_total, gain_total = lax.psum((kernel_part, gain_part), ("dp", "red"))
    return (
        module_output,
        frame_gradient,
        grad_weights * grad_scale,
        kernel_total * grad_scale,
        gain_total * grad_scale,
    )


def solution(mesh):
    placed = (
        P(("dp", "red"), None, None),
        P(("dp", "red"), None, None),
        P("red", None),
        P(),
        P(),
        P(),
    )
    return jax.shard_map(
        local,
        mesh=mesh,
        in_specs=placed,
        out_specs=(
            P(("dp", "red"), None, None),
            P(("dp", "red"), None, None),
            P("red", None),
            P(),
            P(),
        ),
        check_vma=False,
    )
```

profile of v0, /device:TPU:1, one launch (start us, length us, event | category | flops | bytes accessed | tf_op | source)
XLA Modules:
  0.0 923.5 jit_solution(477016552205187638)
XLA Ops:
  8.8 2.1 convert_reduce_fusion
  12.2 2.2 fusion.11
  14.4 8.3 copy.13
  22.7 10.7 %reshape_reshape.3 = bf16[768,8,16,12]{0,3,2,1:T(8,128)(2,1)} reshape(bf16[16,48,1536]{1,0,2:T(8,128)(2,1)} %copy.13) | data formatting | bytes 4718592 | tf_op jit(solution)/shard_map/reshape;reshape | solution.py:101
  33.4 4.0 copy.14
  37.4 5.2 reshape.139
  43.8 23.9 %all-gather.4.cloned.1.call-done = bf16[1536,3072]{1,0:T(8,128)(2,1)} async-done(((bf16[192,3072]{1,0:T(8,128)(2,1)}), bf16[1536,3072]{1,0:T(8,128)(2,1)}) %all-gather.4.cloned.1.call-update) | async-done | bytes 9437200 | tf_op jit(solution)/shard_map/all_gather | solution.py:88
  67.7 10.8 %fusion.3 = f32[16,48,3072]{2,1,0:T(8,128)S(1)} fusion(bf16[16,48,1536]{2,1,0:T(8,128)(2,1)} %fusion.11, bf16[1536,3072]{1,0:T(8,128)(2,1)} %all-gather.4.cloned.1.call-done), kind=kOutput, calls=%fused_computation.62 | convolution fusion | flops 7247757312 | bytes 21233664 | tf_op jit(solution)/shard_map/dot_general | solution.py:23
  79.9 2.7 copy-done.3
  82.6 49.2 %multiply_reduce_fusion = (f32[1536]{0:T(1024)}, f32[1536]{0:T(1024)}, f32[1536]{0:T(1024)}, f32[1536]{0:T(1024)}, f32[1536]{0:T(1024)}, /*index=5*/f32[1536]{0:...) fusion(f32[16,48,1536]{2,1,0:T(8,128)S(1)} %multiply_multiply_f, ...), kind=kLoop, calls=%fused_computation.186 | loop fusion | flops 150981120 | bytes 16856064 | tf_op jit(solution)/shard_map/reduce_sum | solution.py:50
  132.0 28.6 %multiply_convert_fusion.1 = (bf16[16,48,1536]{2,1,0:T(8,128)(2,1)S(1)}, f32[16,48,1536]{2,1,0:T(8,128)}) fusion(f32[16,48,3072]{2,1,0:T(8,128)} %copy-done.3, f32[16,48]{1,0:T(8,128)S(1)} %get-tuple-element.106, f32[16,48]{1,0:T(8,128)S(1)} %get-tuple-element.76, f32[1536]{0:T(1024)} %copy-done.57, f32[16,48]{1,0:T(8,128)S(1)} %get-tuple-element.77, ...), kind=kLoop, calls=%fused_computation.218 | loop fusion | flops 114425856 | bytes 16800768 | tf_op jit(solution)/shard_map/convert.4
  160.6 6.9 multiply_convert_fusion
  168.9 10.8 %fusion.119 = f32[1536,3072]{1,0:T(8,128)} fusion(bf16[768,1536]{0,1:T(8,128)(2,1)S(1)} %copy-done.8, bf16[768,1536]{1,0:T(8,128)(2,1)S(1)} %bitcast.24, bf16[768,1536]{1,0:T(8,128)(2,1)S(1)} %bitcast.23), kind=kOutput, calls=%fused_computation.182 | convolution fusion | flops 7257194496 | bytes 25952256 | tf_op jit(solution)/shard_map/dot_general | solution.py:104
  179.8 359.8 %fusion = f32[16,3072]{1,0:T(8,128)S(1)} fusion(f32[1536,3072]{1,0:T(8,128)} %fusion.119), kind=kCustom, calls=%all-reduce-scatter | all-reduce-scatter fusion | flops 6291457 | bytes 19070976
  552.0 15.3 %collective-permute-start.22 = (f32[16,3072]{1,0:T(8,128)S(1)}, f32[16,3072]{1,0:T(8,128)S(1)}, u32[]{:S(2)}, u32[]{:S(2)}) collective-permute-start(f32[16,3072]{1,0:T(8,128)S(1)} %fusion), channel_id=1, source_target_pairs={{0,23},{1,24},{2,25},{3,26},{4,27},{5,28},{6,29},{7,30},{8,31},{9,... | collective-permute-start | bytes 589832
  567.3 6.4 collective-permute-start.21
  573.7 5.7 collective-permute-start.20
  579.4 8.4 collective-permute-start.19
  587.8 2.0 collective-permute-start.18
  589.8 5.9 collective-permute-start.17
  595.7 2.0 collective-permute-start.16
  597.7 3.8 collective-permute-start.15
  603.1 5.5 collective-permute-start.14
  608.6 12.3 %collective-permute-start.13 = (f32[16,3072]{1,0:T(8,128)S(1)}, f32[16,3072]{1,0:T(8,128)S(1)}, u32[]{:S(2)}, u32[]{:S(2)}) collective-permute-start(f32[16,3072]{1,0:T(8,128)S(1)} %fusion), channel_id=1, source_target_pairs={{0,14},{1,15},{2,16},{3,17},{4,18},{5,19},{6,20},{7,21},{8,22},{9,... | collective-permute-start | bytes 589832
  620.9 10.3 %collective-permute-start.12 = (f32[16,3072]{1,0:T(8,128)S(1)}, f32[16,3072]{1,0:T(8,128)S(1)}, u32[]{:S(2)}, u32[]{:S(2)}) collective-permute-start(f32[16,3072]{1,0:T(8,128)S(1)} %fusion), channel_id=1, source_target_pairs={{0,13},{1,14},{2,15},{3,16},{4,17},{5,18},{6,19},{7,20},{8,21},{9,... | collective-permute-start | bytes 589832
  631.2 14.7 %collective-permute-start.11 = (f32[16,3072]{1,0:T(8,128)S(1)}, f32[16,3072]{1,0:T(8,128)S(1)}, u32[]{:S(2)}, u32[]{:S(2)}) collective-permute-start(f32[16,3072]{1,0:T(8,128)S(1)} %fusion), channel_id=1, source_target_pairs={{0,12},{1,13},{2,14},{3,15},{4,16},{5,17},{6,18},{7,19},{8,20},{9,... | collective-permute-start | bytes 589832
  647.3 26.0 %multiply_reduce_fusion.9 = (f32[1536]{0:T(1024)S(1)}, f32[1536]{0:T(1024)S(1)}, f32[1536]{0:T(1024)S(1)}, f32[1536]{0:T(1024)S(1)}, f32[1536]{0:T(1024)S(1)}, /...) fusion(f32[16,48,1536]{2,1,0:T(8,128)} %copy-done.1, f32[16,48,1536]{2,1,0:T(8,128)} %copy-done, ...), kind=kLoop, calls=%fused_computation.195 | loop fusion | flops 30657024 | bytes 9517056 | tf_op jit(solution)/shard_map/reduce_sum | solution.py:50
  674.6 5.2 collective-permute-start.8
  679.9 1.9 collective-permute-start.7
  681.8 2.5 collective-permute-start.6
  685.1 2.7 collective-permute-start.5
  687.9 9.0 multiply_reduce_fusion.18
  697.0 6.7 collective-permute-start.4
  703.7 2.0 collective-permute-start.3
  705.7 4.6 collective-permute-start.2
  710.3 2.0 collective-permute-start.1
  712.9 2.1 collective-permute-start
  715.0 3.9 multiply_reduce_fusion.27
  719.5 2.7 stack.127
  722.4 84.8 %concatenate.17 = f32[524,3072]{1,0:T(8,128)} concatenate(f32[12,3072]{1,0:T(8,128)S(1)} %collective-permute-done.31, f32[16,3072]{1,0:T(8,128)S(1)} %collective-permute-done.30, f32[16,3072]{1,0:T(8,128)} %copy-done.9, f32[16,3072]{1,0:T(8,128)} %copy-done.10, f32[16,3072]{1,0:T(8,128)} %copy-done.11, f32[16,3072]{1,0:T(8,128)} %copy-done.12, f32[16,3072]{1,0:T(8,128)} %copy-done.13, ...), dimensions={0} | concatenate | bytes 12877824
  807.2 1.7 dynamic-slice_bitcast_fusion
  808.9 14.3 %fusion.18 = (f32[1536]{0:T(1024)S(1)}, f32[16,48]{1,0:T(8,128)S(1)}, f32[16,48]{1,0:T(8,128)S(1)}, f32[16,48,1536]{2,1,0:T(8,128)}) fusion(bf16[16,48,1536]{2,1,0:T(8,128)(2,1)S(1)} %copy-done.4, f32[16,48]{1,0:T(8,128)S(1)} %copy-done.60, f32[16,48]{1,0:T(8,128)S(1)} %copy-done.52, f32[1536]{0:T(1024)S(1)} %copy-done.62, ...), kind=kOutput, calls=%fused_computation.80 | convolution fusion | flops 7267808256 | bytes 21258240 | tf_op jit(solution)/shard_map/dot_general | solution.py:67
  823.2 63.9 %psum.15 = f32[1536]{0:T(1024)S(1)} all-reduce(f32[1536]{0:T(1024)S(1)} %get-tuple-element.36), channel_id=1, replica_groups=mesh['dp'=16,'red'=8] {'dp','red'}, use_global_device_ids=true, to_apply=%region_39.40 | all-reduce | flops 1536 | bytes 12288 | tf_op jit(solution)/shard_map/psum | solution.py:112
  887.7 7.8 fusion.17
  895.6 1.6 broadcast_multiply_fusion.1
  897.2 12.9 %all-gather.6.cloned.1.call-done = f32[16,12,3072]{2,1,0:T(8,128)} async-done(((f32[1,12,3072]{2,1,0:T(8,128)}), f32[16,12,3072]{2,1,0:T(8,128)}) %all-gather.6.cloned.1.call-update) | async-done | bytes 2359312 | tf_op jit(solution)/shard_map/all_gather | solution.py:111
  910.1 3.9 broadcast_multiply_fusion
  914.0 3.0 reshape.143
  (248 shorter events, 24.7 us)
Async XLA Ops:
  7.2 60.5 %all-gather.4.cloned.1.call-start = ((), (), s32[]{:S(2)}) async-start(), calls=%async_computation | async-start | bytes 10616832 | tf_op jit(solution)/shard_map/all_gather | solution.py:88
  7.9 887.6 %all-reduce.7.cloned.1.call-start = ((), (), s32[]{:S(2)}) async-start(), calls=%async_computation.1 | async-start | bytes 393216 | tf_op jit(solution)/shard_map/psum | solution.py:112
  43.5 88.4 %copy-start.42 = (f32[16,48]{1,0:T(8,128)}, f32[16,48]{1,0:T(8,128)S(1)}, u32[]{:S(2)}) copy-start(f32[16,48]{1,0:T(8,128)S(1)} %get-tuple-element.89) | copy-start | bytes 9220
  43.5 88.4 %copy-start.44 = (f32[16,48]{1,0:T(8,128)}, f32[16,48]{1,0:T(8,128)S(1)}, u32[]{:S(2)}) copy-start(f32[16,48]{1,0:T(8,128)S(1)} %get-tuple-element.90) | copy-start | bytes 9220
  43.5 88.4 %copy-start.45 = (f32[16,48]{1,0:T(8,128)}, f32[16,48]{1,0:T(8,128)S(1)}, u32[]{:S(2)}) copy-start(f32[16,48]{1,0:T(8,128)S(1)} %get-tuple-element.91) | copy-start | bytes 9220
  43.5 88.4 %copy-start.46 = (f32[16,48]{1,0:T(8,128)}, f32[16,48]{1,0:T(8,128)S(1)}, u32[]{:S(2)}) copy-start(f32[16,48]{1,0:T(8,128)S(1)} %get-tuple-element.92) | copy-start | bytes 9220
  43.5 88.4 %copy-start.47 = (f32[16,48]{1,0:T(8,128)}, f32[16,48]{1,0:T(8,128)S(1)}, u32[]{:S(2)}) copy-start(f32[16,48]{1,0:T(8,128)S(1)} %get-tuple-element.93) | copy-start | bytes 9220
  43.6 88.3 %copy-start.48 = (f32[16,48]{1,0:T(8,128)}, f32[16,48]{1,0:T(8,128)S(1)}, u32[]{:S(2)}) copy-start(f32[16,48]{1,0:T(8,128)S(1)} %get-tuple-element.94) | copy-start | bytes 9220
  43.6 88.3 %copy-start.49 = (f32[16,48]{1,0:T(8,128)}, f32[16,48]{1,0:T(8,128)S(1)}, u32[]{:S(2)}) copy-start(f32[16,48]{1,0:T(8,128)S(1)} %get-tuple-element.95) | copy-start | bytes 9220
  43.6 88.3 %copy-start.50 = (f32[16,48]{1,0:T(8,128)}, f32[16,48]{1,0:T(8,128)S(1)}, u32[]{:S(2)}) copy-start(f32[16,48]{1,0:T(8,128)S(1)} %get-tuple-element.96) | copy-start | bytes 9220
  43.7 88.2 %copy-start.30 = (f32[16,48]{1,0:T(8,128)}, f32[16,48]{1,0:T(8,128)S(1)}, u32[]{:S(2)}) copy-start(f32[16,48]{1,0:T(8,128)S(1)} %get-tuple-element.79) | copy-start | bytes 9220
  43.7 88.2 %copy-start.32 = (f32[16,48]{1,0:T(8,128)}, f32[16,48]{1,0:T(8,128)S(1)}, u32[]{:S(2)}) copy-start(f32[16,48]{1,0:T(8,128)S(1)} %get-tuple-element.80) | copy-start | bytes 9220
  43.8 88.2 %copy-start.34 = (f32[16,48]{1,0:T(8,128)}, f32[16,48]{1,0:T(8,128)S(1)}, u32[]{:S(2)}) copy-start(f32[16,48]{1,0:T(8,128)S(1)} %get-tuple-element.81) | copy-start | bytes 9220
  179.7 421.8 %copy-start.72 = (s32[2048]{0:T(1024)S(1)}, s32[2048]{0:T(1024)}, u32[]{:S(2)}) copy-start(s32[2048]{0:T(1024)} %param.11) | copy-start | bytes 24580
  179.7 467.5 %copy-start.43 = (f32[16,48]{1,0:T(8,128)S(1)}, f32[16,48]{1,0:T(8,128)}, u32[]{:S(2)}) copy-start(f32[16,48]{1,0:T(8,128)} %copy-done.42) | copy-start | bytes 9220
  539.6 7.9 collective-permute-start.30
  540.9 5.2 collective-permute-start.31
  542.2 6.6 collective-permute-start.29
  543.5 6.6 collective-permute-start.28
  544.9 7.2 collective-permute-start.27
  546.2 21.1 %collective-permute-start.26 = (f32[16,3072]{1,0:T(8,128)S(1)}, f32[16,3072]{1,0:T(8,128)S(1)}, u32[]{:S(2)}, u32[]{:S(2)}) collective-permute-start(f32[16,3072]{1,0:T(8,128)S(1)} %fusion), channel_id=1, source_target_pairs={{0,27},{1,28},{2,29},{3,30},{4,31},{5,32},{6,33},{7,34},{8,35},{9,... | collective-permute-start | bytes 589832
  547.5 26.2 %collective-permute-start.25 = (f32[16,3072]{1,0:T(8,128)S(1)}, f32[16,3072]{1,0:T(8,128)S(1)}, u32[]{:S(2)}, u32[]{:S(2)}) collective-permute-start(f32[16,3072]{1,0:T(8,128)S(1)} %fusion), channel_id=1, source_target_pairs={{0,26},{1,27},{2,28},{3,29},{4,30},{5,31},{6,32},{7,33},{8,34},{9,... | collective-permute-start | bytes 589832
  548.8 30.6 %collective-permute-start.24 = (f32[16,3072]{1,0:T(8,128)S(1)}, f32[16,3072]{1,0:T(8,128)S(1)}, u32[]{:S(2)}, u32[]{:S(2)}) collective-permute-start(f32[16,3072]{1,0:T(8,128)S(1)} %fusion), channel_id=1, source_target_pairs={{0,25},{1,26},{2,27},{3,28},{4,29},{5,30},{6,31},{7,32},{8,33},{9,... | collective-permute-start | bytes 589832
  550.2 37.6 %collective-permute-start.23 = (f32[16,3072]{1,0:T(8,128)S(1)}, f32[16,3072]{1,0:T(8,128)S(1)}, u32[]{:S(2)}, u32[]{:S(2)}) collective-permute-start(f32[16,3072]{1,0:T(8,128)S(1)} %fusion), channel_id=1, source_target_pairs={{0,24},{1,25},{2,26},{3,27},{4,28},{5,29},{6,30},{7,31},{8,32},{9,... | collective-permute-start | bytes 589832
  552.0 37.8 %collective-permute-start.22 = (f32[16,3072]{1,0:T(8,128)S(1)}, f32[16,3072]{1,0:T(8,128)S(1)}, u32[]{:S(2)}, u32[]{:S(2)}) collective-permute-start(f32[16,3072]{1,0:T(8,128)S(1)} %fusion), channel_id=1, source_target_pairs={{0,23},{1,24},{2,25},{3,26},{4,27},{5,28},{6,29},{7,30},{8,31},{9,... | collective-permute-start | bytes 589832
  567.3 28.4 %collective-permute-start.21 = (f32[16,3072]{1,0:T(8,128)S(1)}, f32[16,3072]{1,0:T(8,128)S(1)}, u32[]{:S(2)}, u32[]{:S(2)}) collective-permute-start(f32[16,3072]{1,0:T(8,128)S(1)} %fusion), channel_id=1, source_target_pairs={{0,22},{1,23},{2,24},{3,25},{4,26},{5,27},{6,28},{7,29},{8,30},{9,... | collective-permute-start | bytes 589832
  573.7 24.0 %collective-permute-start.20 = (f32[16,3072]{1,0:T(8,128)S(1)}, f32[16,3072]{1,0:T(8,128)S(1)}, u32[]{:S(2)}, u32[]{:S(2)}) collective-permute-start(f32[16,3072]{1,0:T(8,128)S(1)} %fusion), channel_id=1, source_target_pairs={{0,21},{1,22},{2,23},{3,24},{4,25},{5,26},{6,27},{7,28},{8,29},{9,... | collective-permute-start | bytes 589832
  579.4 23.7 %collective-permute-start.19 = (f32[16,3072]{1,0:T(8,128)S(1)}, f32[16,3072]{1,0:T(8,128)}, u32[]{:S(2)}, u32[]{:S(2)}) collective-permute-start(f32[16,3072]{1,0:T(8,128)S(1)} %fusion), channel_id=1, source_target_pairs={{0,20},{1,21},{2,22},{3,23},{4,24},{5,25},{6,26},{7,27},{8,28},{9,... | collective-permute-start | bytes 589832
  587.8 20.8 %collective-permute-start.18 = (f32[16,3072]{1,0:T(8,128)S(1)}, f32[16,3072]{1,0:T(8,128)}, u32[]{:S(2)}, u32[]{:S(2)}) collective-permute-start(f32[16,3072]{1,0:T(8,128)S(1)} %fusion), channel_id=1, source_target_pairs={{0,19},{1,20},{2,21},{3,22},{4,23},{5,24},{6,25},{7,26},{8,27},{9,... | collective-permute-start | bytes 589832
  589.8 31.1 %collective-permute-start.17 = (f32[16,3072]{1,0:T(8,128)S(1)}, f32[16,3072]{1,0:T(8,128)}, u32[]{:S(2)}, u32[]{:S(2)}) collective-permute-start(f32[16,3072]{1,0:T(8,128)S(1)} %fusion), channel_id=1, source_target_pairs={{0,18},{1,19},{2,20},{3,21},{4,22},{5,23},{6,24},{7,25},{8,26},{9,... | collective-permute-start | bytes 589832
  595.7 35.5 %collective-permute-start.16 = (f32[16,3072]{1,0:T(8,128)S(1)}, f32[16,3072]{1,0:T(8,128)}, u32[]{:S(2)}, u32[]{:S(2)}) collective-permute-start(f32[16,3072]{1,0:T(8,128)S(1)} %fusion), channel_id=1, source_target_pairs={{0,17},{1,18},{2,19},{3,20},{4,21},{5,22},{6,23},{7,24},{8,25},{9,... | collective-permute-start | bytes 589832
  597.7 48.2 %collective-permute-start.15 = (f32[16,3072]{1,0:T(8,128)S(1)}, f32[16,3072]{1,0:T(8,128)}, u32[]{:S(2)}, u32[]{:S(2)}) collective-permute-start(f32[16,3072]{1,0:T(8,128)S(1)} %fusion), channel_id=1, source_target_pairs={{0,16},{1,17},{2,18},{3,19},{4,20},{5,21},{6,22},{7,23},{8,24},{9,... | collective-permute-start | bytes 589832
  603.1 70.1 %collective-permute-start.14 = (f32[16,3072]{1,0:T(8,128)S(1)}, f32[16,3072]{1,0:T(8,128)S(1)}, u32[]{:S(2)}, u32[]{:S(2)}) collective-permute-start(f32[16,3072]{1,0:T(8,128)S(1)} %fusion), channel_id=1, source_target_pairs={{0,15},{1,16},{2,17},{3,18},{4,19},{5,20},{6,21},{7,22},{8,23},{9,... | collective-permute-start | bytes 589832
  608.6 65.9 %collective-permute-start.13 = (f32[16,3072]{1,0:T(8,128)S(1)}, f32[16,3072]{1,0:T(8,128)S(1)}, u32[]{:S(2)}, u32[]{:S(2)}) collective-permute-start(f32[16,3072]{1,0:T(8,128)S(1)} %fusion), channel_id=1, source_target_pairs={{0,14},{1,15},{2,16},{3,17},{4,18},{5,19},{6,20},{7,21},{8,22},{9,... | collective-permute-start | bytes 589832
  620.9 58.9 %collective-permute-start.12 = (f32[16,3072]{1,0:T(8,128)S(1)}, f32[16,3072]{1,0:T(8,128)S(1)}, u32[]{:S(2)}, u32[]{:S(2)}) collective-permute-start(f32[16,3072]{1,0:T(8,128)S(1)} %fusion), channel_id=1, source_target_pairs={{0,13},{1,14},{2,15},{3,16},{4,17},{5,18},{6,19},{7,20},{8,21},{9,... | collective-permute-start | bytes 589832
  631.2 50.6 %collective-permute-start.11 = (f32[16,3072]{1,0:T(8,128)S(1)}, f32[16,3072]{1,0:T(8,128)S(1)}, u32[]{:S(2)}, u32[]{:S(2)}) collective-permute-start(f32[16,3072]{1,0:T(8,128)S(1)} %fusion), channel_id=1, source_target_pairs={{0,12},{1,13},{2,14},{3,15},{4,16},{5,17},{6,18},{7,19},{8,20},{9,... | collective-permute-start | bytes 589832
  646.0 38.4 %collective-permute-start.10 = (f32[16,3072]{1,0:T(8,128)S(1)}, f32[16,3072]{1,0:T(8,128)S(1)}, u32[]{:S(2)}, u32[]{:S(2)}) collective-permute-start(f32[16,3072]{1,0:T(8,128)S(1)} %fusion), channel_id=1, source_target_pairs={{0,11},{1,12},{2,13},{3,14},{4,15},{5,16},{6,17},{7,18},{8,19},{9,... | collective-permute-start | bytes 589832
  673.3 23.7 %collective-permute-start.9 = (f32[16,3072]{1,0:T(8,128)S(1)}, f32[16,3072]{1,0:T(8,128)S(1)}, u32[]{:S(2)}, u32[]{:S(2)}) collective-permute-start(f32[16,3072]{1,0:T(8,128)S(1)} %fusion), channel_id=1, source_target_pairs={{0,10},{1,11},{2,12},{3,13},{4,14},{5,15},{6,16},{7,17},{8,18},{9,... | collective-permute-start | bytes 589832
  674.6 29.1 %collective-permute-start.8 = (f32[16,3072]{1,0:T(8,128)S(1)}, f32[16,3072]{1,0:T(8,128)S(1)}, u32[]{:S(2)}, u32[]{:S(2)}) collective-permute-start(f32[16,3072]{1,0:T(8,128)S(1)} %fusion), channel_id=1, source_target_pairs={{0,9},{1,10},{2,11},{3,12},{4,13},{5,14},{6,15},{7,16},{8,17},{9,1... | collective-permute-start | bytes 589832
  679.9 25.8 %collective-permute-start.7 = (f32[16,3072]{1,0:T(8,128)S(1)}, f32[16,3072]{1,0:T(8,128)S(1)}, u32[]{:S(2)}, u32[]{:S(2)}) collective-permute-start(f32[16,3072]{1,0:T(8,128)S(1)} %fusion), channel_id=1, source_target_pairs={{0,8},{1,9},{2,10},{3,11},{4,12},{5,13},{6,14},{7,15},{8,16},{9,17... | collective-permute-start | bytes 589832
  681.8 28.5 %collective-permute-start.6 = (f32[16,3072]{1,0:T(8,128)S(1)}, f32[16,3072]{1,0:T(8,128)S(1)}, u32[]{:S(2)}, u32[]{:S(2)}) collective-permute-start(f32[16,3072]{1,0:T(8,128)S(1)} %fusion), channel_id=1, source_target_pairs={{0,7},{1,8},{2,9},{3,10},{4,11},{5,12},{6,13},{7,14},{8,15},{9,16}... | collective-permute-start | bytes 589832
  685.1 27.1 %collective-permute-start.5 = (f32[16,3072]{1,0:T(8,128)S(1)}, f32[16,3072]{1,0:T(8,128)S(1)}, u32[]{:S(2)}, u32[]{:S(2)}) collective-permute-start(f32[16,3072]{1,0:T(8,128)S(1)} %fusion), channel_id=1, source_target_pairs={{0,6},{1,7},{2,8},{3,9},{4,10},{5,11},{6,12},{7,13},{8,14},{9,15},... | collective-permute-start | bytes 589832
  697.0 25.4 %collective-permute-start.4 = (f32[16,3072]{1,0:T(8,128)S(1)}, f32[16,3072]{1,0:T(8,128)}, u32[]{:S(2)}, u32[]{:S(2)}) collective-permute-start(f32[16,3072]{1,0:T(8,128)S(1)} %fusion), channel_id=1, source_target_pairs={{0,5},{1,6},{2,7},{3,8},{4,9},{5,10},{6,11},{7,12},{8,13},{9,14},{... | collective-permute-start | bytes 589832
  703.7 18.6 %collective-permute-start.3 = (f32[16,3072]{1,0:T(8,128)S(1)}, f32[16,3072]{1,0:T(8,128)}, u32[]{:S(2)}, u32[]{:S(2)}) collective-permute-start(f32[16,3072]{1,0:T(8,128)S(1)} %fusion), channel_id=1, source_target_pairs={{0,4},{1,5},{2,6},{3,7},{4,8},{5,9},{6,10},{7,11},{8,12},{9,13},{1... | collective-permute-start | bytes 589832
  705.7 16.7 %collective-permute-start.2 = (f32[16,3072]{1,0:T(8,128)S(1)}, f32[16,3072]{1,0:T(8,128)}, u32[]{:S(2)}, u32[]{:S(2)}) collective-permute-start(f32[16,3072]{1,0:T(8,128)S(1)} %fusion), channel_id=1, source_target_pairs={{0,3},{1,4},{2,5},{3,6},{4,7},{5,8},{6,9},{7,10},{8,11},{9,12},{10... | collective-permute-start | bytes 589832
  710.3 12.1 %collective-permute-start.1 = (f32[16,3072]{1,0:T(8,128)S(1)}, f32[16,3072]{1,0:T(8,128)}, u32[]{:S(2)}, u32[]{:S(2)}) collective-permute-start(f32[16,3072]{1,0:T(8,128)S(1)} %fusion), channel_id=1, source_target_pairs={{0,2},{1,3},{2,4},{3,5},{4,6},{5,7},{6,8},{7,9},{8,10},{9,11},{10,... | collective-permute-start | bytes 589832
  712.9 9.5 %collective-permute-start = (f32[16,3072]{1,0:T(8,128)S(1)}, f32[16,3072]{1,0:T(8,128)}, u32[]{:S(2)}, u32[]{:S(2)}) collective-permute-start(f32[16,3072]{1,0:T(8,128)S(1)} %fusion), channel_id=1, source_target_pairs={{0,1},{1,2},{2,3},{3,4},{4,5},{5,6},{6,7},{7,8},{8,9},{9,10},{10,1... | collective-permute-start | bytes 589832
  722.3 187.8 %all-gather.6.cloned.1.call-start = ((), (), s32[]{:S(2)}) async-start(), calls=%async_computation.2 | async-start | bytes 3342336 | tf_op jit(solution)/shard_map/all_gather | solution.py:111
  (62 other events, 2134.4 us)
Sparse Core Ops, SparseCore 0:
  9.7 57.9 all-gather.3
  722.4 139.3 all-reduce.6
  864.2 45.8 all-gather.5
where the time goes:
time: 927 us; the launch traced here: 924 us
  blocking collectives  424 us (46%)
  other arithmetic  145 us (16%)
  starting transfers between devices  136 us (15%)
  local copies, waits for them, and re-layouts  128 us (14%)
  waiting for transfers between devices  38.2 us (4%)
  matrix products  35.9 us (4%)
  between operations  16.2 us (2%)
    unnamed x1, blocking collectives  360 us
    unnamed x32, starting transfers between devices  136 us
    unnamed x153, local copies, waits for them, and re-layouts  92.8 us
    reduce_sum x4, other arithmetic, block_pass(): kernel_terms.append(jnp.sum(grad_conv * window * same_seg, axis=(0, 1)))  88.1 us
    psum x1, blocking collectives, local(): kernel_total, gain_total = lax.psum((kernel_part, gain_part), ('dp', 'red'))  63.9 us
    another operation x2, other arithmetic  35.5 us
    all_gather x1, waiting for transfers between devices, local(): weights = lax.all_gather(w_in, 'red', axis=0, tiled=True)  23.9 us
  transfers between devices with their start and end apart: 35, of which 3 were waited for; matrix products, arithmetic and copies ran while one was open for 20% of the time, Pallas kernels for 0%

commit v1 on v0

--- a/solution.py
+++ b/solution.py
@@ -1,9 +1,17 @@
+import functools
 import jax
 import jax.numpy as jnp
 from jax import lax
 from jax.sharding import PartitionSpec as P
 
 EPSILON = 1e-05
+
+
+def _do_sizes(raw, axis_tag, chip_axis):
+    return lax.psum(lax.psum(raw, axis_tag), chip_axis)
+
+
+frames_edit = functools.partial(_do_sizes, axis_tag="dp", chip_axis="red")
 
 
 def normalize(widened_frames):
@@ -109,7 +117,7 @@
         tiled=True,
     )
     grad_weights = lax.all_gather(owned_rows, "dp", axis=0, tiled=True)
-    kernel_total, gain_total = lax.psum((kernel_part, gain_part), ("dp", "red"))
+    kernel_total, gain_total = frames_edit((kernel_part, gain_part))
     return (
         module_output,
         frame_gradient,

time: 927 us -> 995 us (1.073)
  waiting for transfers between devices: 38.2 us -> 106 us
  blocking collectives: 424 us -> 413 us
    psum x1 -> x2, waiting for transfers between devices: 0.01 us -> 80 us  [_do_sizes(): return lax.psum(lax.psum(raw, axis_tag), chip_axis)]
    all_gather x1, waiting for transfers between devices: 12.9 us -> 0.01 us  [local(): grad_weights = lax.all_gather(owned_rows, 'dp', axis=0, tiled=True)]
    psum x1 -> x2, blocking collectives: 63.9 us -> 53 us  [_do_sizes(): return lax.psum(lax.psum(raw, axis_tag), chip_axis)]
    unnamed x153 -> x177, local copies, waits for them, and re-layouts: 92.8 us -> 93.3 us
  transfers between devices with their start and end apart: 35 -> 36, of which waited for: 3 -> 3; matrix products, arithmetic and copies ran while one was open for 20% -> 20% of each run, Pallas kernels for 0% -> 0%
where the time goes in v1:
time: 995 us; the launch traced here: 991 us
  blocking collectives  413 us (42%)
  other arithmetic  147 us (15%)
  starting transfers between devices  139 us (14%)
  local copies, waits for them, and re-layouts  134 us (13%)
  waiting for transfers between devices  106 us (11%)
  matrix products  35.9 us (4%)
  between operations  16.4 us (2%)
    unnamed x1, blocking collectives  360 us
    unnamed x32, starting transfers between devices  139 us
    unnamed x177, local copies, waits for them, and re-layouts  93.3 us
    reduce_sum x4, other arithmetic, block_pass(): kernel_terms.append(jnp.sum(grad_conv * window * same_seg, axis=(0, 1)))  89.1 us
    psum x2, waiting for transfers between devices, _do_sizes(): return lax.psum(lax.psum(raw, axis_tag), chip_axis)  80 us
    psum x2, blocking collectives, _do_sizes(): return lax.psum(lax.psum(raw, axis_tag), chip_axis)  53 us
    another operation x2, other arithmetic  35.5 us
    all_gather x1, waiting for transfers between devices, local(): weights = lax.all_gather(w_in, 'red', axis=0, tiled=True)  23.9 us
  transfers between devices with their start and end apart: 36, of which 3 were waited for; matrix products, arithmetic and copies ran while one was open for 20% of the time, Pallas kernels for 0%

profile of v1, /device:TPU:1, one launch (start us, length us, event | category | flops | bytes accessed | tf_op | source)
XLA Modules:
  0.0 990.9 jit_solution(7184912724434476179)
XLA Ops:
  8.8 2.1 convert_reduce_fusion
  12.2 2.2 fusion.11
  14.4 8.3 copy.13
  22.7 10.7 %reshape_reshape.3 = bf16[768,8,16,12]{0,3,2,1:T(8,128)(2,1)} reshape(bf16[16,48,1536]{1,0,2:T(8,128)(2,1)} %copy.13) | data formatting | bytes 4718592 | tf_op jit(solution)/shard_map/reshape;reshape | solution.py:109
  33.4 4.0 copy.14
  37.4 5.2 reshape.139
  43.8 23.9 %all-gather.4.cloned.1.call-done = bf16[1536,3072]{1,0:T(8,128)(2,1)} async-done(((bf16[192,3072]{1,0:T(8,128)(2,1)}), bf16[1536,3072]{1,0:T(8,128)(2,1)}) %all-gather.4.cloned.1.call-update) | async-done | bytes 9437200 | tf_op jit(solution)/shard_map/all_gather | solution.py:96
  67.7 10.8 %fusion.3 = f32[16,48,3072]{2,1,0:T(8,128)S(1)} fusion(bf16[16,48,1536]{2,1,0:T(8,128)(2,1)} %fusion.11, bf16[1536,3072]{1,0:T(8,128)(2,1)} %all-gather.4.cloned.1.call-done), kind=kOutput, calls=%fused_computation.62 | convolution fusion | flops 7247757312 | bytes 21233664 | tf_op jit(solution)/shard_map/dot_general | solution.py:31
  79.9 2.7 copy-done.2
  82.6 49.2 %multiply_reduce_fusion = (f32[1536]{0:T(1024)}, f32[1536]{0:T(1024)}, f32[1536]{0:T(1024)}, f32[1536]{0:T(1024)}, f32[1536]{0:T(1024)}, /*index=5*/f32[1536]{0:...) fusion(f32[16,48,1536]{2,1,0:T(8,128)S(1)} %multiply_multiply_f, ...), kind=kLoop, calls=%fused_computation.186 | loop fusion | flops 150981120 | bytes 16856064 | tf_op jit(solution)/shard_map/reduce_sum | solution.py:58
  132.0 28.6 %multiply_convert_fusion.1 = (bf16[16,48,1536]{2,1,0:T(8,128)(2,1)S(1)}, f32[16,48,1536]{2,1,0:T(8,128)}) fusion(f32[16,48,3072]{2,1,0:T(8,128)} %copy-done.2, f32[16,48]{1,0:T(8,128)S(1)} %get-tuple-element.106, f32[16,48]{1,0:T(8,128)S(1)} %get-tuple-element.76, f32[1536]{0:T(1024)} %copy-done.68, f32[16,48]{1,0:T(8,128)S(1)} %get-tuple-element.77, ...), kind=kLoop, calls=%fused_computation.218 | loop fusion | flops 114425856 | bytes 16800768 | tf_op jit(solution)/shard_map/convert.4
  160.6 6.9 multiply_convert_fusion
  168.9 10.8 %fusion.119 = f32[1536,3072]{1,0:T(8,128)} fusion(bf16[768,1536]{0,1:T(8,128)(2,1)S(1)} %copy-done.7, bf16[768,1536]{1,0:T(8,128)(2,1)S(1)} %bitcast.26, bf16[768,1536]{1,0:T(8,128)(2,1)S(1)} %bitcast.25), kind=kOutput, calls=%fused_computation.182 | convolution fusion | flops 7257194496 | bytes 25952256 | tf_op jit(solution)/shard_map/dot_general | solution.py:112
  179.8 359.8 %fusion = f32[16,3072]{1,0:T(8,128)S(1)} fusion(f32[1536,3072]{1,0:T(8,128)} %fusion.119), kind=kCustom, calls=%all-reduce-scatter | all-reduce-scatter fusion | flops 6291457 | bytes 19070976
  541.1 1.6 collective-permute-start.31
  552.7 15.0 %collective-permute-start.22 = (f32[16,3072]{1,0:T(8,128)S(1)}, f32[16,3072]{1,0:T(8,128)S(1)}, u32[]{:S(2)}, u32[]{:S(2)}) collective-permute-start(f32[16,3072]{1,0:T(8,128)S(1)} %fusion), channel_id=1, source_target_pairs={{0,23},{1,24},{2,25},{3,26},{4,27},{5,28},{6,29},{7,30},{8,31},{9,... | collective-permute-start | bytes 589832
  567.7 6.4 collective-permute-start.21
  574.1 5.7 collective-permute-start.20
  579.8 7.7 collective-permute-start.19
  588.9 6.6 collective-permute-start.17
  596.9 4.3 collective-permute-start.15
  601.2 5.9 collective-permute-start.14
  607.1 12.3 %collective-permute-start.13 = (f32[16,3072]{1,0:T(8,128)S(1)}, f32[16,3072]{1,0:T(8,128)S(1)}, u32[]{:S(2)}, u32[]{:S(2)}) collective-permute-start(f32[16,3072]{1,0:T(8,128)S(1)} %fusion), channel_id=1, source_target_pairs={{0,14},{1,15},{2,16},{3,17},{4,18},{5,19},{6,20},{7,21},{8,22},{9,... | collective-permute-start | bytes 589832
  619.4 10.3 %collective-permute-start.12 = (f32[16,3072]{1,0:T(8,128)S(1)}, f32[16,3072]{1,0:T(8,128)S(1)}, u32[]{:S(2)}, u32[]{:S(2)}) collective-permute-start(f32[16,3072]{1,0:T(8,128)S(1)} %fusion), channel_id=1, source_target_pairs={{0,13},{1,14},{2,15},{3,16},{4,17},{5,18},{6,19},{7,20},{8,21},{9,... | collective-permute-start | bytes 589832
  629.8 14.7 %collective-permute-start.11 = (f32[16,3072]{1,0:T(8,128)S(1)}, f32[16,3072]{1,0:T(8,128)S(1)}, u32[]{:S(2)}, u32[]{:S(2)}) collective-permute-start(f32[16,3072]{1,0:T(8,128)S(1)} %fusion), channel_id=1, source_target_pairs={{0,12},{1,13},{2,14},{3,15},{4,16},{5,17},{6,18},{7,19},{8,20},{9,... | collective-permute-start | bytes 589832
  646.7 26.1 %multiply_reduce_fusion.9 = (f32[1536]{0:T(1024)S(1)}, f32[1536]{0:T(1024)S(1)}, f32[1536]{0:T(1024)S(1)}, f32[1536]{0:T(1024)S(1)}, f32[1536]{0:T(1024)S(1)}, /...) fusion(f32[16,48,1536]{2,1,0:T(8,128)} %copy-done.1, f32[16,48,1536]{2,1,0:T(8,128)} %copy-done, ...), kind=kLoop, calls=%fused_computation.195 | loop fusion | flops 30657024 | bytes 9517056 | tf_op jit(solution)/shard_map/reduce_sum | solution.py:58
  674.3 5.2 collective-permute-start.8
  679.5 1.9 collective-permute-start.7
  681.5 2.5 collective-permute-start.6
  684.7 3.5 collective-permute-start.5
  688.2 9.8 multiply_reduce_fusion.18
  698.2 5.9 collective-permute-start.4
  704.1 2.0 collective-permute-start.3
  706.1 6.9 collective-permute-start.2
  713.1 2.2 collective-permute-start.1
  716.0 2.7 collective-permute-start
  718.8 3.9 multiply_reduce_fusion.27
  727.3 4.2 stack.127
  733.7 80.0 %all-reduce.8.cloned.1.call-done = f32[31,1536]{1,0:T(8,128)} async-done(((f32[31,1536]{1,0:T(8,128)}), f32[31,1536]{1,0:T(8,128)}) %all-reduce.8.cloned.1.call-update) | async-done | bytes 190480 | tf_op jit(solution)/shard_map/psum | solution.py:11
  813.8 84.6 %concatenate.17 = f32[524,3072]{1,0:T(8,128)} concatenate(f32[12,3072]{1,0:T(8,128)S(1)} %collective-permute-done.31, f32[16,3072]{1,0:T(8,128)S(1)} %collective-permute-done.30, f32[16,3072]{1,0:T(8,128)S(1)} %collective-permute-done.29, f32[16,3072]{1,0:T(8,128)S(1)} %copy-done.9, f32[16,3072]{1,0:T(8,128)} %copy-done.10, f32[16,3072]{1,0:T(8,128)} %copy-done.11, ...), dimensions={0} | concatenate | bytes 12877824
  898.4 1.7 dynamic-slice_bitcast_fusion
  900.1 14.3 %fusion.18 = (f32[1536]{0:T(1024)S(1)}, f32[16,48]{1,0:T(8,128)S(1)}, f32[16,48]{1,0:T(8,128)S(1)}, f32[16,48,1536]{2,1,0:T(8,128)}) fusion(bf16[16,48,1536]{2,1,0:T(8,128)(2,1)S(1)} %copy-done.3, f32[16,48]{1,0:T(8,128)S(1)} %copy-done.71, f32[16,48]{1,0:T(8,128)S(1)} %copy-done.63, f32[1536]{0:T(1024)S(1)} %copy-done.73, ...), kind=kOutput, calls=%fused_computation.80 | convolution fusion | flops 7267808256 | bytes 21258240 | tf_op jit(solution)/shard_map/dot_general | solution.py:75
  914.4 31.9 %psum.30 = f32[1536]{0:T(1024)S(1)} all-reduce(f32[1536]{0:T(1024)S(1)} %get-tuple-element.36), channel_id=1, replica_groups=mesh['dp'=16,'red'=8] {'dp'}, use_global_device_ids=true, to_apply=%region_40.41 | all-reduce | flops 1536 | bytes 12288 | tf_op jit(solution)/shard_map/psum | solution.py:11
  946.2 21.1 %psum.31 = f32[1536]{0:T(1024)S(1)} all-reduce(f32[1536]{0:T(1024)S(1)} %psum.30), channel_id=1, replica_groups=mesh['dp'=16,'red'=8] {'red'}, use_global_device_ids=true, to_apply=%region_41.42 | all-reduce | flops 1536 | bytes 12288 | tf_op jit(solution)/shard_map/psum | solution.py:11
  968.0 7.8 fusion.17
  975.8 1.6 broadcast_multiply_fusion.1
  977.4 3.9 broadcast_multiply_fusion
  981.3 3.0 reshape.143
  (277 shorter events, 32.1 us)
Async XLA Ops:
  7.2 60.5 %all-gather.4.cloned.1.call-start = ((), (), s32[]{:S(2)}) async-start(), calls=%async_computation | async-start | bytes 10616832 | tf_op jit(solution)/shard_map/all_gather | solution.py:96
  7.9 805.7 %all-reduce.8.cloned.1.call-start = ((), (), s32[]{:S(2)}) async-start(), calls=%async_computation.1 | async-start | bytes 393216 | tf_op jit(solution)/shard_map/psum | solution.py:11
  179.7 466.8 %copy-start.47 = (f32[16,48]{1,0:T(8,128)S(1)}, f32[16,48]{1,0:T(8,128)}, u32[]{:S(2)}) copy-start(f32[16,48]{1,0:T(8,128)} %copy-done.46) | copy-start | bytes 9220
  179.7 466.8 %copy-start.49 = (f32[16,48]{1,0:T(8,128)S(1)}, f32[16,48]{1,0:T(8,128)}, u32[]{:S(2)}) copy-start(f32[16,48]{1,0:T(8,128)} %copy-done.48) | copy-start | bytes 9220
  179.8 466.9 %copy-start.51 = (f32[16,48]{1,0:T(8,128)S(1)}, f32[16,48]{1,0:T(8,128)}, u32[]{:S(2)}) copy-start(f32[16,48]{1,0:T(8,128)} %copy-done.50) | copy-start | bytes 9220
  179.8 466.9 %copy-start.53 = (f32[16,48]{1,0:T(8,128)S(1)}, f32[16,48]{1,0:T(8,128)}, u32[]{:S(2)}) copy-start(f32[16,48]{1,0:T(8,128)} %copy-done.52) | copy-start | bytes 9220
  179.8 466.9 %copy-start.55 = (f32[16,48]{1,0:T(8,128)S(1)}, f32[16,48]{1,0:T(8,128)}, u32[]{:S(2)}) copy-start(f32[16,48]{1,0:T(8,128)} %copy-done.54) | copy-start | bytes 9220
  179.8 466.9 %copy-start.57 = (f32[16,48]{1,0:T(8,128)S(1)}, f32[16,48]{1,0:T(8,128)}, u32[]{:S(2)}) copy-start(f32[16,48]{1,0:T(8,128)} %copy-done.56) | copy-start | bytes 9220
  179.8 466.9 %copy-start.59 = (f32[16,48]{1,0:T(8,128)S(1)}, f32[16,48]{1,0:T(8,128)}, u32[]{:S(2)}) copy-start(f32[16,48]{1,0:T(8,128)} %copy-done.58) | copy-start | bytes 9220
  179.8 466.9 %copy-start.61 = (f32[16,48]{1,0:T(8,128)S(1)}, f32[16,48]{1,0:T(8,128)}, u32[]{:S(2)}) copy-start(f32[16,48]{1,0:T(8,128)} %copy-done.60) | copy-start | bytes 9220
  539.7 8.2 collective-permute-start.30
  541.0 147.2 %slice-start = ((s8[4718592]{0:T(1024)(128)(4,1)}), s8[4194304]{0:T(1024)(128)(4,1)S(1)}, s32[]{:S(2)}) async-start(s8[4718592]{0:T(1024)(128)(4,1)} %bitcast.20), calls=%async_computation.4 | async-start | bytes 8388608
  541.0 147.2 %slice-start.1 = ((s8[4718592]{0:T(1024)(128)(4,1)}), s8[524288]{0:T(1024)(128)(4,1)S(1)}, s32[]{:S(2)}) async-start(s8[4718592]{0:T(1024)(128)(4,1)} %bitcast.20), calls=%async_computation.5 | async-start | bytes 1048576
  541.0 147.2 %copy-start.37 = (f32[16,48]{1,0:T(8,128)S(1)}, f32[16,48]{1,0:T(8,128)}, u32[]{:S(2)}) copy-start(f32[16,48]{1,0:T(8,128)} %copy-done.36) | copy-start | bytes 9220
  541.0 147.2 %copy-start.39 = (f32[16,48]{1,0:T(8,128)S(1)}, f32[16,48]{1,0:T(8,128)}, u32[]{:S(2)}) copy-start(f32[16,48]{1,0:T(8,128)} %copy-done.38) | copy-start | bytes 9220
  541.1 5.5 collective-permute-start.31
  542.6 6.6 collective-permute-start.29
  543.9 6.6 collective-permute-start.28
  545.2 7.5 collective-permute-start.27
  546.6 21.1 %collective-permute-start.26 = (f32[16,3072]{1,0:T(8,128)S(1)}, f32[16,3072]{1,0:T(8,128)S(1)}, u32[]{:S(2)}, u32[]{:S(2)}) collective-permute-start(f32[16,3072]{1,0:T(8,128)S(1)} %fusion), channel_id=1, source_target_pairs={{0,27},{1,28},{2,29},{3,30},{4,31},{5,32},{6,33},{7,34},{8,35},{9,... | collective-permute-start | bytes 589832
  547.9 26.2 %collective-permute-start.25 = (f32[16,3072]{1,0:T(8,128)S(1)}, f32[16,3072]{1,0:T(8,128)S(1)}, u32[]{:S(2)}, u32[]{:S(2)}) collective-permute-start(f32[16,3072]{1,0:T(8,128)S(1)} %fusion), channel_id=1, source_target_pairs={{0,26},{1,27},{2,28},{3,29},{4,30},{5,31},{6,32},{7,33},{8,34},{9,... | collective-permute-start | bytes 589832
  549.2 30.6 %collective-permute-start.24 = (f32[16,3072]{1,0:T(8,128)S(1)}, f32[16,3072]{1,0:T(8,128)S(1)}, u32[]{:S(2)}, u32[]{:S(2)}) collective-permute-start(f32[16,3072]{1,0:T(8,128)S(1)} %fusion), channel_id=1, source_target_pairs={{0,25},{1,26},{2,27},{3,28},{4,29},{5,30},{6,31},{7,32},{8,33},{9,... | collective-permute-start | bytes 589832
  550.5 37.0 %collective-permute-start.23 = (f32[16,3072]{1,0:T(8,128)S(1)}, f32[16,3072]{1,0:T(8,128)S(1)}, u32[]{:S(2)}, u32[]{:S(2)}) collective-permute-start(f32[16,3072]{1,0:T(8,128)S(1)} %fusion), channel_id=1, source_target_pairs={{0,24},{1,25},{2,26},{3,27},{4,28},{5,29},{6,30},{7,31},{8,32},{9,... | collective-permute-start | bytes 589832
  552.7 36.1 %collective-permute-start.22 = (f32[16,3072]{1,0:T(8,128)S(1)}, f32[16,3072]{1,0:T(8,128)S(1)}, u32[]{:S(2)}, u32[]{:S(2)}) collective-permute-start(f32[16,3072]{1,0:T(8,128)S(1)} %fusion), channel_id=1, source_target_pairs={{0,23},{1,24},{2,25},{3,26},{4,27},{5,28},{6,29},{7,30},{8,31},{9,... | collective-permute-start | bytes 589832
  567.7 27.8 %collective-permute-start.21 = (f32[16,3072]{1,0:T(8,128)S(1)}, f32[16,3072]{1,0:T(8,128)S(1)}, u32[]{:S(2)}, u32[]{:S(2)}) collective-permute-start(f32[16,3072]{1,0:T(8,128)S(1)} %fusion), channel_id=1, source_target_pairs={{0,22},{1,23},{2,24},{3,25},{4,26},{5,27},{6,28},{7,29},{8,30},{9,... | collective-permute-start | bytes 589832
  574.1 22.8 %collective-permute-start.20 = (f32[16,3072]{1,0:T(8,128)S(1)}, f32[16,3072]{1,0:T(8,128)S(1)}, u32[]{:S(2)}, u32[]{:S(2)}) collective-permute-start(f32[16,3072]{1,0:T(8,128)S(1)} %fusion), channel_id=1, source_target_pairs={{0,21},{1,22},{2,23},{3,24},{4,25},{5,26},{6,27},{7,28},{8,29},{9,... | collective-permute-start | bytes 589832
  579.8 21.4 %collective-permute-start.19 = (f32[16,3072]{1,0:T(8,128)S(1)}, f32[16,3072]{1,0:T(8,128)S(1)}, u32[]{:S(2)}, u32[]{:S(2)}) collective-permute-start(f32[16,3072]{1,0:T(8,128)S(1)} %fusion), channel_id=1, source_target_pairs={{0,20},{1,21},{2,22},{3,23},{4,24},{5,25},{6,26},{7,27},{8,28},{9,... | collective-permute-start | bytes 589832
  587.6 19.6 %collective-permute-start.18 = (f32[16,3072]{1,0:T(8,128)S(1)}, f32[16,3072]{1,0:T(8,128)S(1)}, u32[]{:S(2)}, u32[]{:S(2)}) collective-permute-start(f32[16,3072]{1,0:T(8,128)S(1)} %fusion), channel_id=1, source_target_pairs={{0,19},{1,20},{2,21},{3,22},{4,23},{5,24},{6,25},{7,26},{8,27},{9,... | collective-permute-start | bytes 589832
  588.9 30.5 %collective-permute-start.17 = (f32[16,3072]{1,0:T(8,128)S(1)}, f32[16,3072]{1,0:T(8,128)S(1)}, u32[]{:S(2)}, u32[]{:S(2)}) collective-permute-start(f32[16,3072]{1,0:T(8,128)S(1)} %fusion), channel_id=1, source_target_pairs={{0,18},{1,19},{2,20},{3,21},{4,22},{5,23},{6,24},{7,25},{8,26},{9,... | collective-permute-start | bytes 589832
  595.6 34.2 %collective-permute-start.16 = (f32[16,3072]{1,0:T(8,128)S(1)}, f32[16,3072]{1,0:T(8,128)S(1)}, u32[]{:S(2)}, u32[]{:S(2)}) collective-permute-start(f32[16,3072]{1,0:T(8,128)S(1)} %fusion), channel_id=1, source_target_pairs={{0,17},{1,18},{2,19},{3,20},{4,21},{5,22},{6,23},{7,24},{8,25},{9,... | collective-permute-start | bytes 589832
  596.9 47.6 %collective-permute-start.15 = (f32[16,3072]{1,0:T(8,128)S(1)}, f32[16,3072]{1,0:T(8,128)S(1)}, u32[]{:S(2)}, u32[]{:S(2)}) collective-permute-start(f32[16,3072]{1,0:T(8,128)S(1)} %fusion), channel_id=1, source_target_pairs={{0,16},{1,17},{2,18},{3,19},{4,20},{5,21},{6,22},{7,23},{8,24},{9,... | collective-permute-start | bytes 589832
  601.2 71.5 %collective-permute-start.14 = (f32[16,3072]{1,0:T(8,128)S(1)}, f32[16,3072]{1,0:T(8,128)S(1)}, u32[]{:S(2)}, u32[]{:S(2)}) collective-permute-start(f32[16,3072]{1,0:T(8,128)S(1)} %fusion), channel_id=1, source_target_pairs={{0,15},{1,16},{2,17},{3,18},{4,19},{5,20},{6,21},{7,22},{8,23},{9,... | collective-permute-start | bytes 589832
  607.1 67.1 %collective-permute-start.13 = (f32[16,3072]{1,0:T(8,128)S(1)}, f32[16,3072]{1,0:T(8,128)S(1)}, u32[]{:S(2)}, u32[]{:S(2)}) collective-permute-start(f32[16,3072]{1,0:T(8,128)S(1)} %fusion), channel_id=1, source_target_pairs={{0,14},{1,15},{2,16},{3,17},{4,18},{5,19},{6,20},{7,21},{8,22},{9,... | collective-permute-start | bytes 589832
  619.4 60.1 %collective-permute-start.12 = (f32[16,3072]{1,0:T(8,128)S(1)}, f32[16,3072]{1,0:T(8,128)S(1)}, u32[]{:S(2)}, u32[]{:S(2)}) collective-permute-start(f32[16,3072]{1,0:T(8,128)S(1)} %fusion), channel_id=1, source_target_pairs={{0,13},{1,14},{2,15},{3,16},{4,17},{5,18},{6,19},{7,20},{8,21},{9,... | collective-permute-start | bytes 589832
  629.8 51.7 %collective-permute-start.11 = (f32[16,3072]{1,0:T(8,128)S(1)}, f32[16,3072]{1,0:T(8,128)S(1)}, u32[]{:S(2)}, u32[]{:S(2)}) collective-permute-start(f32[16,3072]{1,0:T(8,128)S(1)} %fusion), channel_id=1, source_target_pairs={{0,12},{1,13},{2,14},{3,15},{4,16},{5,17},{6,18},{7,19},{8,20},{9,... | collective-permute-start | bytes 589832
  645.3 38.7 %collective-permute-start.10 = (f32[16,3072]{1,0:T(8,128)S(1)}, f32[16,3072]{1,0:T(8,128)S(1)}, u32[]{:S(2)}, u32[]{:S(2)}) collective-permute-start(f32[16,3072]{1,0:T(8,128)S(1)} %fusion), channel_id=1, source_target_pairs={{0,11},{1,12},{2,13},{3,14},{4,15},{5,16},{6,17},{7,18},{8,19},{9,... | collective-permute-start | bytes 589832
  672.8 25.4 %collective-permute-start.9 = (f32[16,3072]{1,0:T(8,128)S(1)}, f32[16,3072]{1,0:T(8,128)S(1)}, u32[]{:S(2)}, u32[]{:S(2)}) collective-permute-start(f32[16,3072]{1,0:T(8,128)S(1)} %fusion), channel_id=1, source_target_pairs={{0,10},{1,11},{2,12},{3,13},{4,14},{5,15},{6,16},{7,17},{8,18},{9,... | collective-permute-start | bytes 589832
  674.3 29.9 %collective-permute-start.8 = (f32[16,3072]{1,0:T(8,128)S(1)}, f32[16,3072]{1,0:T(8,128)S(1)}, u32[]{:S(2)}, u32[]{:S(2)}) collective-permute-start(f32[16,3072]{1,0:T(8,128)S(1)} %fusion), channel_id=1, source_target_pairs={{0,9},{1,10},{2,11},{3,12},{4,13},{5,14},{6,15},{7,16},{8,17},{9,1... | collective-permute-start | bytes 589832
  679.5 26.6 %collective-permute-start.7 = (f32[16,3072]{1,0:T(8,128)S(1)}, f32[16,3072]{1,0:T(8,128)S(1)}, u32[]{:S(2)}, u32[]{:S(2)}) collective-permute-start(f32[16,3072]{1,0:T(8,128)S(1)} %fusion), channel_id=1, source_target_pairs={{0,8},{1,9},{2,10},{3,11},{4,12},{5,13},{6,14},{7,15},{8,16},{9,17... | collective-permute-start | bytes 589832
  681.5 31.6 %collective-permute-start.6 = (f32[16,3072]{1,0:T(8,128)S(1)}, f32[16,3072]{1,0:T(8,128)S(1)}, u32[]{:S(2)}, u32[]{:S(2)}) collective-permute-start(f32[16,3072]{1,0:T(8,128)S(1)} %fusion), channel_id=1, source_target_pairs={{0,7},{1,8},{2,9},{3,10},{4,11},{5,12},{6,13},{7,14},{8,15},{9,16}... | collective-permute-start | bytes 589832
  684.7 30.6 %collective-permute-start.5 = (f32[16,3072]{1,0:T(8,128)S(1)}, f32[16,3072]{1,0:T(8,128)S(1)}, u32[]{:S(2)}, u32[]{:S(2)}) collective-permute-start(f32[16,3072]{1,0:T(8,128)S(1)} %fusion), channel_id=1, source_target_pairs={{0,6},{1,7},{2,8},{3,9},{4,10},{5,11},{6,12},{7,13},{8,14},{9,15},... | collective-permute-start | bytes 589832
  698.2 115.5 %collective-permute-start.4 = (f32[16,3072]{1,0:T(8,128)S(1)}, f32[16,3072]{1,0:T(8,128)}, u32[]{:S(2)}, u32[]{:S(2)}) collective-permute-start(f32[16,3072]{1,0:T(8,128)S(1)} %fusion), channel_id=1, source_target_pairs={{0,5},{1,6},{2,7},{3,8},{4,9},{5,10},{6,11},{7,12},{8,13},{9,14},{... | collective-permute-start | bytes 589832
  704.1 109.6 %collective-permute-start.3 = (f32[16,3072]{1,0:T(8,128)S(1)}, f32[16,3072]{1,0:T(8,128)}, u32[]{:S(2)}, u32[]{:S(2)}) collective-permute-start(f32[16,3072]{1,0:T(8,128)S(1)} %fusion), channel_id=1, source_target_pairs={{0,4},{1,5},{2,6},{3,7},{4,8},{5,9},{6,10},{7,11},{8,12},{9,13},{1... | collective-permute-start | bytes 589832
  706.1 107.6 %collective-permute-start.2 = (f32[16,3072]{1,0:T(8,128)S(1)}, f32[16,3072]{1,0:T(8,128)}, u32[]{:S(2)}, u32[]{:S(2)}) collective-permute-start(f32[16,3072]{1,0:T(8,128)S(1)} %fusion), channel_id=1, source_target_pairs={{0,3},{1,4},{2,5},{3,6},{4,7},{5,8},{6,9},{7,10},{8,11},{9,12},{10... | collective-permute-start | bytes 589832
  713.1 100.7 %collective-permute-start.1 = (f32[16,3072]{1,0:T(8,128)S(1)}, f32[16,3072]{1,0:T(8,128)}, u32[]{:S(2)}, u32[]{:S(2)}) collective-permute-start(f32[16,3072]{1,0:T(8,128)S(1)} %fusion), channel_id=1, source_target_pairs={{0,2},{1,3},{2,4},{3,5},{4,6},{5,7},{6,8},{7,9},{8,10},{9,11},{10,... | collective-permute-start | bytes 589832
  716.0 97.7 %collective-permute-start = (f32[16,3072]{1,0:T(8,128)S(1)}, f32[16,3072]{1,0:T(8,128)}, u32[]{:S(2)}, u32[]{:S(2)}) collective-permute-start(f32[16,3072]{1,0:T(8,128)S(1)} %fusion), channel_id=1, source_target_pairs={{0,1},{1,2},{2,3},{3,4},{4,5},{5,6},{6,7},{7,8},{8,9},{9,10},{10,1... | collective-permute-start | bytes 589832
  731.5 244.3 %all-reduce.10.cloned.1.call-start = ((), (), s32[]{:S(2)}) async-start(), calls=%async_computation.2 | async-start | bytes 393216 | tf_op jit(solution)/shard_map/psum | solution.py:11
  813.7 163.8 %all-gather.6.cloned.1.call-start = ((), (), s32[]{:S(2)}) async-start(), calls=%async_computation.3 | async-start | bytes 3342336 | tf_op jit(solution)/shard_map/all_gather | solution.py:119
  (75 other events, 3624.0 us)
Sparse Core Ops, SparseCore 0:
  9.7 57.9 all-gather.3
  731.7 81.9 all-reduce.7
  815.9 58.5 all-reduce.9
  900.2 48.5 all-gather.5
